TPU v7x, 128 devices: a whole 4x4x4 slice. The times are simulated.
128 devices in a mesh: row: 8 (over y_lo, x), col: 16 (over z, y_hi, core).
Axes of the slice: x: 4, y: 4 (y_hi: 2, y_lo: 2; y = y_hi * 2 + y_lo), z: 4, core: 2. Of those that a mesh axis runs over, the one named last changes fastest.
Arguments:
- hidden_in: bfloat16 [2048, 8192], P('col', 'row'), may hold values from -130 to 130
- norm_gain: float32 [8192], P('row'), may hold values from 0.5 to 1.5
- w_query: bfloat16 [8192, 8192], P('row', 'col'), may hold values from -0.0625 to 0.0625
- scale_query: float32 [64, 64], P('row', 'col'), may hold values from 0.35 to 2.8
- bias_query: float32 [8192], P('col'), may hold values from -14 to 14
- w_keyval: bfloat16 [8192, 2048], P('row'), may hold values from -0.0625 to 0.0625
- scale_keyval: float32 [64, 16], P('row'), may hold values from 0.35 to 2.8
- bias_keyval: float32 [2048], replicated, may hold values from -3 to 3
- w_out: bfloat16 [8192, 8192], P('col', 'row'), may hold values from -0.0625 to 0.0625
- scale_out: float32 [64, 64], P('col', 'row'), may hold values from 0.35 to 2.8
- cache_keyval: bfloat16 [2, 8192, 1024], P(None, 'row'), may hold values from -14 to 14
- span_offset: int32 [1], replicated, may hold values from 2048 to 8192
Outputs:
- hidden_out: bfloat16 [2048, 8192], P('col', 'row')
All inputs are finite; a program needn't handle non-finite values.
Results may differ from a plain program's by a relative error of at most 0.033.
Values may be sent and summed in bfloat16 or wider, within the bound.
No kernel may reach another device: no remote copies, remote signals or barrier semaphores. Data moves between devices by JAX's collectives and lax.ppermute only.
A program may use at most 192 MiB of HBM per device.

v0:
```python
import math
import jax
import jax.numpy as jnp
from jax import lax
from jax.sharding import PartitionSpec as P

D = 8192
H = 64
KVH = 8
HD = 128
QB = 128
EPSILON = 1e-06
ROPE_BASE = 1000000.0
MASKED = -1e30


def dequantize(weight, block_scale):
    expanded = jnp.repeat(jnp.repeat(block_scale, QB, axis=0), QB, axis=1)
    return (weight.astype(jnp.float32) * expanded).astype(jnp.bfloat16)


def rotate(vectors, positions):
    half_dim = HD // 2
    inverse = ROPE_BASE ** (-(2.0 * jnp.arange(half_dim, dtype=jnp.float32)) / HD)
    angles = positions[:, None] * inverse[None, :]
    cosine = jnp.cos(angles)[:, None, :]
    sine_part = jnp.sin(angles)[:, None, :]
    first_half = vectors[..., :half_dim]
    second = vectors[..., half_dim:]
    return jnp.concatenate(
        [first_half * cosine - second * sine_part, second * cosine + first_half * sine_part],
        axis=-1,
    )


def block_scores(queries, key_block, key_index, query_index, offset, cache_len):
    scores = jnp.einsum("thd,kd->htk", queries, key_block, preferred_element_type=jnp.float32) * (
        1.0 / math.sqrt(HD)
    )
    earlier = (key_index < cache_len)[None, :]
    allowed = jnp.where(
        earlier,
        (key_index < offset)[None, :],
        (key_index - cache_len)[None, :] <= query_index[:, None],
    )
    return jnp.where(allowed[None, :, :], scores, MASKED)


def score_blocks(queries, key_rows, key_index, query_index, offset, cache_len, block_len):
    key_blocks = key_rows.reshape(-1, block_len, key_rows.shape[-1])
    index_blocks = key_index.reshape(-1, block_len)

    def one_block(block_item):
        return block_scores(queries, block_item[0], block_item[1], query_index, offset, cache_len)

    return lax.map(one_block, (key_blocks, index_blocks))


def block_stats(scores):
    row_peak = jnp.max(scores, axis=(0, 3))
    weights = jnp.where(scores > 0.5 * MASKED, jnp.exp(scores - row_peak[None, :, :, None]), 0.0)
    return (row_peak, jnp.sum(weights, axis=(0, 3)))


def weighted_values(scores, value_rows, block_len, row_peak, row_total):
    value_blocks = value_rows.reshape(-1, block_len, value_rows.shape[-1])

    def advance(summed, block_item):
        weights = (jnp.exp(block_item[0] - row_peak[:, :, None]) / row_total[:, :, None]).astype(
            jnp.bfloat16
        )
        return (
            summed
            + jnp.einsum("htk,kd->thd", weights, block_item[1], preferred_element_type=jnp.float32),
            None,
        )

    start_state = jnp.zeros((scores.shape[2], scores.shape[1], HD), jnp.float32)
    return lax.scan(advance, start_state, (scores, value_blocks))[0]


def body(
    hidden_in,
    norm_gain,
    w_query,
    scale_query,
    bias_query,
    w_keyval,
    scale_keyval,
    bias_keyval,
    w_out,
    scale_out,
    cache_keyval,
    span_offset,
):
    row_count = lax.axis_size("row")
    row_index = lax.axis_index("row")
    col_index = lax.axis_index("col")
    widened = hidden_in.astype(jnp.float32)
    squares = lax.psum(jnp.sum(widened * widened, axis=1), "row")
    norm_ratio = lax.rsqrt(squares / D + EPSILON)
    normed = (widened * norm_ratio[:, None] * norm_gain[None, :]).astype(jnp.bfloat16)
    gathered = lax.all_gather(normed, "col", axis=0, tiled=True)
    tokens = gathered.shape[0]
    tok_dev = tokens // row_count
    heads_dev = w_query.shape[1] // HD
    qwidth = heads_dev * HD
    group_size = H // KVH
    kv_width = KVH * HD
    kv_head = col_index * heads_dev // group_size
    key_cols = lax.dynamic_slice_in_dim(w_keyval, kv_head * HD, HD, 1)
    value_cols = lax.dynamic_slice_in_dim(w_keyval, kv_width + kv_head * HD, HD, 1)
    key_scale = lax.dynamic_slice_in_dim(scale_keyval, kv_head * (HD // QB), HD // QB, 1)
    value_scale = lax.dynamic_slice_in_dim(
        scale_keyval, (kv_width + kv_head * HD) // QB, HD // QB, 1
    )
    combined = jnp.concatenate(
        [
            dequantize(w_query, scale_query),
            dequantize(key_cols, key_scale),
            dequantize(value_cols, value_scale),
        ],
        axis=1,
    )
    projected = lax.psum_scatter(
        jnp.dot(gathered, combined, preferred_element_type=jnp.float32).astype(jnp.bfloat16),
        "row",
        scatter_dimension=0,
        tiled=True,
    ).astype(jnp.float32)
    bias_key = lax.dynamic_slice_in_dim(bias_keyval, kv_head * HD, HD, 0)
    bias_value = lax.dynamic_slice_in_dim(bias_keyval, kv_width + kv_head * HD, HD, 0)
    offset = span_offset[0]
    query_index = row_index * tok_dev + jnp.arange(tok_dev, dtype=jnp.int32)
    positions = (offset + query_index).astype(jnp.float32)
    queries = rotate(
        (projected[:, :qwidth] + bias_query[None, :]).reshape(tok_dev, heads_dev, HD), positions
    ).astype(jnp.bfloat16)
    own_keys = rotate(
        (projected[:, qwidth : qwidth + HD] + bias_key[None, :]).reshape(tok_dev, 1, HD), positions
    )
    own_keys = own_keys.reshape(tok_dev, HD).astype(jnp.bfloat16)
    own_values = (projected[:, qwidth + HD :] + bias_value[None, :]).astype(jnp.bfloat16)
    span_kv = lax.all_gather(
        jnp.concatenate([own_keys, own_values], axis=1), "row", axis=0, tiled=True
    )
    span_keys = span_kv[:, :HD]
    span_values = span_kv[:, HD:]
    cache_dev = cache_keyval.shape[1]
    cache_len = cache_dev * row_count
    cache_head = lax.dynamic_slice_in_dim(cache_keyval, kv_head * HD, HD, 2)
    span_index = cache_len + jnp.arange(tokens, dtype=jnp.int32)
    all_queries = lax.all_gather(
        queries.reshape(tok_dev, qwidth), "row", axis=0, tiled=True
    ).reshape(tokens, heads_dev, HD)
    every_index = jnp.arange(tokens, dtype=jnp.int32)
    cache_index = row_index * cache_dev + jnp.arange(cache_dev, dtype=jnp.int32)
    cache_scores = score_blocks(
        all_queries, cache_head[0], cache_index, every_index, offset, cache_len, tok_dev
    )
    cache_peak, cache_total = block_stats(cache_scores)
    own_scores = score_blocks(
        queries, span_keys, span_index, query_index, offset, cache_len, tokens
    )
    own_peak, own_total = block_stats(own_scores)
    first_row = row_index * tok_dev
    placed_peak = lax.dynamic_update_slice_in_dim(
        jnp.full_like(cache_peak, MASKED), own_peak, first_row, 1
    )
    peak_all = lax.pmax(jnp.maximum(cache_peak, placed_peak).astype(jnp.bfloat16), "row").astype(
        jnp.float32
    )
    peak_own = lax.dynamic_slice_in_dim(peak_all, first_row, tok_dev, 1)
    placed_total = lax.dynamic_update_slice_in_dim(
        jnp.zeros_like(cache_total), own_total * jnp.exp(own_peak - peak_own), first_row, 1
    )
    total_all = lax.psum(
        (cache_total * jnp.exp(cache_peak - peak_all) + placed_total).astype(jnp.bfloat16), "row"
    ).astype(jnp.float32)
    total_own = lax.dynamic_slice_in_dim(total_all, first_row, tok_dev, 1)
    cache_part = weighted_values(cache_scores, cache_head[1], tok_dev, peak_all, total_all)
    cache_share = lax.psum_scatter(
        cache_part.reshape(tokens, qwidth).astype(jnp.bfloat16),
        "row",
        scatter_dimension=0,
        tiled=True,
    ).astype(jnp.float32)
    span_part = weighted_values(own_scores, span_values, tokens, peak_own, total_own)
    attended = cache_share.reshape(tok_dev, heads_dev, HD) + span_part
    attended = attended.reshape(tok_dev, qwidth).astype(jnp.bfloat16)
    attention_all = lax.all_gather(attended, "row", axis=0, tiled=True)
    out_weight = dequantize(w_out, scale_out)
    mixed_out = lax.psum_scatter(
        jnp.dot(attention_all, out_weight, preferred_element_type=jnp.float32).astype(jnp.bfloat16),
        "col",
        scatter_dimension=0,
        tiled=True,
    )
    return mixed_out


def solution(mesh):
    return jax.shard_map(
        body,
        mesh=mesh,
        in_specs=(
            P("col", "row"),
            P("row"),
            P("row", "col"),
            P("row", "col"),
            P("col"),
            P("row", None),
            P("row", None),
            P(),
            P("col", "row"),
            P("col", "row"),
            P(None, "row", None),
            P(),
        ),
        out_specs=P("col", "row"),
        check_vma=False,
    )
```

profile of v0, /device:TPU:0, one launch (start us, length us, event | category | flops | bytes accessed | tf_op | source)
XLA Modules:
  0.0 627.0 jit_solution(3063638257543192442)
XLA Ops:
  6.5 1.2 fusion.27
  7.7 19.8 %psum.14 = f32[128]{0:T(128)S(1)} all-reduce(f32[128]{0:T(128)S(1)} %fusion.27), channel_id=1, replica_groups=mesh['row'=8,'col'=16] {'row'}, use_global_device_ids=true, to_apply=%region_1.0 | all-reduce | flops 128 | bytes 1024 | tf_op jit(solution)/shard_map/psum | solution.py:100
  27.5 1.8 fusion.29
  29.4 0.8 copy.28
  30.2 1.0 dynamic-slice_reduce_fusion.1
  31.2 1.4 multiply_convert_fusion.1
  32.7 1.2 broadcast_in_dim.164
  33.9 0.4 fusion.16
  34.3 50.2 %all-gather.5.cloned.1.call-done = bf16[2048,1024]{1,0:T(8,128)(2,1)} async-done(((bf16[128,1024]{1,0:T(8,128)(2,1)}), bf16[2048,1024]{1,0:T(8,128)(2,1)}) %all-gather.5.cloned.1.call-update) | async-done | bytes 4194320 | tf_op jit(solution)/shard_map/all_gather | solution.py:103
  84.6 7.2 %convolution_convert_fusion.1 = bf16[2048,768]{0,1:T(8,128)(2,1)} fusion(bf16[2048,1024]{1,0:T(8,128)(2,1)} %all-gather.5.cloned.1.call-done, bf16[1024,128]{1,0:T(8,128)(2,1)S(1)} %get-tuple-element.263, bf16[1024,128]{1,0:T(8,128)(2,1)S(1)} %get-tuple-element.262, bf16[1024,512]{1,0:T(8,128)(2,1)S(1)} %fusion.16), kind=kOutput, calls=%fused_computation.27 | convolution fusion | flops 3227516928 | bytes 8912896 | tf_op jit(solution)/shard_map/dot_general | solution.py:126
  92.5 0.8 fusion.47
  93.3 42.3 %reduce-scatter.4.cloned.1.call-done = bf16[256,768]{0,1:T(8,128)(2,1)} async-done(((bf16[2048,768]{0,1:T(8,128)(2,1)}), bf16[256,768]{0,1:T(8,128)(2,1)}) %reduce-scatter.4.cloned.1.call-update) | async-done | bytes 393232 | tf_op jit(solution)/shard_map/reduce_scatter | solution.py:125
  135.7 1.0 convert_element_type.105
  136.8 0.3 fusion.38
  137.2 0.7 pad_maximum_fusion
  137.9 0.5 multiply_cosine_fusion
  139.4 0.9 copy.32
  140.2 0.2 reduce-scatter.6.cloned.1.call-start
  140.5 1.1 constant_dynamic-slice_fusion.4
  141.6 1.5 fusion.17
  143.1 31.9 %all-gather.9.cloned.1.call-done = bf16[2048,256]{0,1:T(8,128)(2,1)} async-done(((bf16[256,256]{0,1:T(8,128)(2,1)}), bf16[2048,256]{0,1:T(8,128)(2,1)}) %all-gather.9.cloned.1.call-update) | async-done | bytes 1048592 | tf_op jit(solution)/shard_map/all_gather | solution.py:144
  175.0 2.6 fusion.13
  177.6 3.2 copy-done
  180.8 2.4 select_reduce_fusion.1
  183.1 40.4 %all-gather.7.cloned.1.call-done = bf16[2048,512]{0,1:T(8,128)(2,1)} async-done(((bf16[256,512]{0,1:T(8,128)(2,1)}), bf16[2048,512]{0,1:T(8,128)(2,1)}) %all-gather.7.cloned.1.call-update) | async-done | bytes 2097168 | tf_op jit(solution)/shard_map/all_gather | solution.py:153
  223.5 3.0 copy.33
  226.6 24.4 %while.34 = (s32[]{:T(128)}, f32[4,4,2048,256]{2,3,1,0:T(8,128)}, s32[4,256]{1,0:T(4,128)S(1)}, s32[]{:T(128)}, bf16[4,256,128]{2,1,0:T(8,128)(2,1)S(1)}, /*index=5*/bf16[2048,4,128]{2,0,1:T(8,128)(2,1)S(1)}) while((s32[]{:T(128)}, f32[4,4,2048,256]{2,3,1,0:T(8,128)}, s32[4,256]{1,0:T(4,128)S(1)}, s32[]{:T(128)}, ...), condition=%wide.region_4.5_spmd.clone.clone, body=%wide.region_3.4_spmd.clone.sunk.clone | while | flops 542114560 | bytes 11606097 | solution.py:56
  226.6 0.7 compare_reduce_fusion.4
  227.3 0.6 fusion.64
  227.9 4.8 bitcast_dynamic-update-slice_fusion.3
  232.7 0.7 compare_reduce_fusion.4
  233.4 0.6 fusion.64
  234.0 4.8 bitcast_dynamic-update-slice_fusion.3
  238.8 0.7 compare_reduce_fusion.4
  239.5 0.6 fusion.64
  240.1 4.8 bitcast_dynamic-update-slice_fusion.3
  244.9 0.7 compare_reduce_fusion.4
  245.6 0.6 fusion.64
  246.2 4.8 bitcast_dynamic-update-slice_fusion.3
  250.9 12.0 %reduce_max.18 = f32[4,2048]{1,0:T(4,128)S(1)} reduce(f32[4,4,2048,256]{2,3,1,0:T(8,128)} %get-tuple-element.414, f32[]{:T(128)} %constant.145.clone.1), dimensions={0,3}, to_apply=%region_5.6 | reduce | flops 8380416 | bytes 33587204 | tf_op jit(solution)/shard_map/reduce_max | solution.py:60
  262.9 14.1 %select_reduce_fusion = f32[4,2048]{1,0:T(4,128)S(1)} fusion(f32[4,4,2048,256]{2,3,1,0:T(8,128)} %get-tuple-element.414, f32[4,2048]{1,0:T(4,128)S(1)} %reduce_max.18), kind=kLoop, calls=%fused_computation.20 | loop fusion | flops 33546240 | bytes 33619968 | tf_op jit(solution)/shard_map/reduce_sum | solution.py:62
  277.0 33.2 %pmax.7 = bf16[4,2048]{1,0:T(4,128)(2,1)S(1)} all-reduce(bf16[4,2048]{1,0:T(4,128)(2,1)S(1)} %max.7), channel_id=1, replica_groups=mesh['row'=8,'col'=16] {'row'}, use_global_device_ids=true, to_apply=%region_7.8 | all-reduce | flops 8192 | bytes 32768 | tf_op jit(solution)/shard_map/pmax | solution.py:170
  310.3 30.6 %psum.15 = bf16[4,2048]{1,0:T(4,128)(2,1)S(1)} all-reduce(bf16[4,2048]{1,0:T(4,128)(2,1)S(1)} %convert_element_type.113), channel_id=1, replica_groups=mesh['row'=8,'col'=16] {'row'}, use_global_device_ids=true, to_apply=%region_10.11 | all-reduce | flops 8192 | bytes 32768 | tf_op jit(solution)/shard_map/psum | solution.py:177
  340.9 95.2 %while.35 = (s32[]{:T(128)}, f32[2048,4,128]{0,2,1:T(8,128)}, bf16[4,256,128]{2,1,0:T(8,128)(2,1)S(1)}, f32[4,4,2048,256]{2,3,1,0:T(8,128)}, f32[4,2048]{1,0:T(4,128)S(1)}, /*index=5*/f32[4,2048]{1,0:T(4,128)S(1)}) while((s32[]{:T(128)}, f32[2048,4,128]{0,2,1:T(8,128)}, bf16[4,256,128]{2,1,0:T(8,128)(2,1)S(1)}, ...), condition=%wide.region_12.13_spmd.clone.clone, body=%wide.region_11.12_spmd.clone.sunk.clone | while | flops 545259520 | bytes 50462804 | solution.py:79
  340.9 7.7 %constant_dynamic-slice_fusion.8 = f32[1,4,2048,256]{2,3,1,0:T(8,128)} fusion(f32[4,4,2048,256]{2,3,1,0:T(8,128)} %get-tuple-element.426, s32[]{:T(128)} %get-tuple-element.417), kind=kLoop, calls=%fused_computation.7.clone.1.clone | loop fusion | bytes 16777220 | tf_op jit(solution)/shard_map/while/body/jit(dynamic_index_in_dim)/dynamic_slice | solution.py:79
  348.6 8.7 %copy.53 = f32[1,4,2048,256]{3,2,1,0:T(8,128)} copy(f32[1,4,2048,256]{2,3,1,0:T(8,128)} %constant_dynamic-slice_fusion.8) | data formatting | bytes 16777216 | tf_op jit(solution)/shard_map/while/body/jit(dynamic_index_in_dim)/dynamic_slice | solution.py:79
  357.3 6.8 %bitcast_add_fusion.3 = f32[2048,4,128]{0,2,1:T(8,128)} fusion(f32[2048,4,128]{0,2,1:T(8,128)} %get-tuple-element.418, f32[4,2048]{1,0:T(4,128)S(1)} %get-tuple-element.428, f32[1,4,2048,256]{3,2,1,0:T(8,128)} %copy.53, f32[4,2048]{1,0:T(4,128)S(1)} %get-tuple-element.427, pred[]{:T(512)S(6)} %compare.8, ...), kind=kOutput, calls=%fused_computation.2.clone.1.clone | convolution fusion | flops 545259520 | bytes 16908292 | tf_op jit(solution)/shard_map/while/body/eval_jaxpr/htk,kd->thd/dot_general | solution.py:74
  364.1 7.7 %constant_dynamic-slice_fusion.8 = f32[1,4,2048,256]{2,3,1,0:T(8,128)} fusion(f32[4,4,2048,256]{2,3,1,0:T(8,128)} %get-tuple-element.426, s32[]{:T(128)} %get-tuple-element.417), kind=kLoop, calls=%fused_computation.7.clone.1.clone | loop fusion | bytes 16777220 | tf_op jit(solution)/shard_map/while/body/jit(dynamic_index_in_dim)/dynamic_slice | solution.py:79
  371.8 8.7 %copy.53 = f32[1,4,2048,256]{3,2,1,0:T(8,128)} copy(f32[1,4,2048,256]{2,3,1,0:T(8,128)} %constant_dynamic-slice_fusion.8) | data formatting | bytes 16777216 | tf_op jit(solution)/shard_map/while/body/jit(dynamic_index_in_dim)/dynamic_slice | solution.py:79
  380.5 7.6 %bitcast_add_fusion.3 = f32[2048,4,128]{0,2,1:T(8,128)} fusion(f32[2048,4,128]{0,2,1:T(8,128)} %get-tuple-element.418, f32[4,2048]{1,0:T(4,128)S(1)} %get-tuple-element.428, f32[1,4,2048,256]{3,2,1,0:T(8,128)} %copy.53, f32[4,2048]{1,0:T(4,128)S(1)} %get-tuple-element.427, pred[]{:T(512)S(6)} %compare.8, ...), kind=kOutput, calls=%fused_computation.2.clone.1.clone | convolution fusion | flops 545259520 | bytes 16908292 | tf_op jit(solution)/shard_map/while/body/eval_jaxpr/htk,kd->thd/dot_general | solution.py:74
  388.1 7.7 %constant_dynamic-slice_fusion.8 = f32[1,4,2048,256]{2,3,1,0:T(8,128)} fusion(f32[4,4,2048,256]{2,3,1,0:T(8,128)} %get-tuple-element.426, s32[]{:T(128)} %get-tuple-element.417), kind=kLoop, calls=%fused_computation.7.clone.1.clone | loop fusion | bytes 16777220 | tf_op jit(solution)/shard_map/while/body/jit(dynamic_index_in_dim)/dynamic_slice | solution.py:79
  395.8 8.7 %copy.53 = f32[1,4,2048,256]{3,2,1,0:T(8,128)} copy(f32[1,4,2048,256]{2,3,1,0:T(8,128)} %constant_dynamic-slice_fusion.8) | data formatting | bytes 16777216 | tf_op jit(solution)/shard_map/while/body/jit(dynamic_index_in_dim)/dynamic_slice | solution.py:79
  404.5 7.6 %bitcast_add_fusion.3 = f32[2048,4,128]{0,2,1:T(8,128)} fusion(f32[2048,4,128]{0,2,1:T(8,128)} %get-tuple-element.418, f32[4,2048]{1,0:T(4,128)S(1)} %get-tuple-element.428, f32[1,4,2048,256]{3,2,1,0:T(8,128)} %copy.53, f32[4,2048]{1,0:T(4,128)S(1)} %get-tuple-element.427, pred[]{:T(512)S(6)} %compare.8, ...), kind=kOutput, calls=%fused_computation.2.clone.1.clone | convolution fusion | flops 545259520 | bytes 16908292 | tf_op jit(solution)/shard_map/while/body/eval_jaxpr/htk,kd->thd/dot_general | solution.py:74
  412.2 7.7 %constant_dynamic-slice_fusion.8 = f32[1,4,2048,256]{2,3,1,0:T(8,128)} fusion(f32[4,4,2048,256]{2,3,1,0:T(8,128)} %get-tuple-element.426, s32[]{:T(128)} %get-tuple-element.417), kind=kLoop, calls=%fused_computation.7.clone.1.clone | loop fusion | bytes 16777220 | tf_op jit(solution)/shard_map/while/body/jit(dynamic_index_in_dim)/dynamic_slice | solution.py:79
  419.8 8.7 %copy.53 = f32[1,4,2048,256]{3,2,1,0:T(8,128)} copy(f32[1,4,2048,256]{2,3,1,0:T(8,128)} %constant_dynamic-slice_fusion.8) | data formatting | bytes 16777216 | tf_op jit(solution)/shard_map/while/body/jit(dynamic_index_in_dim)/dynamic_slice | solution.py:79
  428.5 7.6 %bitcast_add_fusion.3 = f32[2048,4,128]{0,2,1:T(8,128)} fusion(f32[2048,4,128]{0,2,1:T(8,128)} %get-tuple-element.418, f32[4,2048]{1,0:T(4,128)S(1)} %get-tuple-element.428, f32[1,4,2048,256]{3,2,1,0:T(8,128)} %copy.53, f32[4,2048]{1,0:T(4,128)S(1)} %get-tuple-element.427, pred[]{:T(512)S(6)} %compare.8, ...), kind=kOutput, calls=%fused_computation.2.clone.1.clone | convolution fusion | flops 545259520 | bytes 16908292 | tf_op jit(solution)/shard_map/while/body/eval_jaxpr/htk,kd->thd/dot_general | solution.py:74
  436.2 3.9 convert_element_type.115
  440.2 41.3 %reduce-scatter.6.cloned.1.call-done = bf16[256,512]{0,1:T(8,128)(2,1)} async-done(((bf16[2048,512]{0,1:T(8,128)(2,1)}), bf16[256,512]{0,1:T(8,128)(2,1)}) %reduce-scatter.6.cloned.1.call-update) | async-done | bytes 262160 | tf_op jit(solution)/shard_map/reduce_scatter | solution.py:182
  481.6 5.7 fusion.25
  487.3 0.3 reduce-scatter.8.cloned.1.call-start
  487.6 44.1 %all-gather.11.cloned.1.call-done = bf16[2048,512]{0,1:T(8,128)(2,1)} async-done(((bf16[256,512]{0,1:T(8,128)(2,1)}), bf16[2048,512]{0,1:T(8,128)(2,1)}) %all-gather.11.cloned.1.call-update) | async-done | bytes 2097168 | tf_op jit(solution)/shard_map/all_gather | solution.py:191
  531.7 0.6 broadcast_in_dim.176
  532.3 6.0 convolution_convert_fusion
  538.3 81.9 %reduce-scatter.8.cloned.1.call-done = bf16[128,1024]{1,0:T(8,128)(2,1)} async-done(((bf16[2048,1024]{1,0:T(8,128)(2,1)}), bf16[128,1024]{1,0:T(8,128)(2,1)}) %reduce-scatter.8.cloned.1.call-update) | async-done | bytes 262160 | tf_op jit(solution)/shard_map/reduce_scatter | solution.py:193
  (55 shorter events, 1.6 us)
Async XLA Ops:
  6.5 27.4 %copy-start.1 = (bf16[1024,512]{1,0:T(8,128)(2,1)S(1)}, bf16[1024,512]{1,0:T(8,128)(2,1)}, u32[]{:S(2)}) copy-start(bf16[1024,512]{1,0:T(8,128)(2,1)} %param.18) | copy-start | bytes 3145732
  6.5 78.0 %all-gather.5.cloned.1.call-start = ((), (), s32[]{:S(2)}) async-start(), calls=%async_computation.3 | async-start | bytes 4456448 | tf_op jit(solution)/shard_map/all_gather | solution.py:103
  29.3 106.3 %reduce-scatter.4.cloned.1.call-start = ((), (), s32[]{:S(2)}) async-start(), calls=%async_computation.4 | async-start | bytes 3538944 | tf_op jit(solution)/shard_map/reduce_scatter | solution.py:125
  91.8 46.6 %copy-start.3 = (f32[512]{0:T(512)S(1)}, f32[512]{0:T(512)}, u32[]{:S(2)}) copy-start(f32[512]{0:T(512)} %param.20) | copy-start | bytes 6148
  91.8 83.2 %all-gather.9.cloned.1.call-start = ((), (), s32[]{:S(2)}) async-start(), calls=%async_computation.6 | async-start | bytes 1179648 | tf_op jit(solution)/shard_map/all_gather | solution.py:144
  137.9 85.7 %all-gather.7.cloned.1.call-start = ((), (), s32[]{:S(2)}) async-start(), calls=%async_computation.5 | async-start | bytes 2359296 | tf_op jit(solution)/shard_map/all_gather | solution.py:153
  140.2 341.3 %reduce-scatter.6.cloned.1.call-start = ((), (), s32[]{:S(2)}) async-start(), calls=%async_computation.7 | async-start | bytes 2359296 | tf_op jit(solution)/shard_map/reduce_scatter | solution.py:182
  177.6 3.2 copy-start
  436.2 45.4 %copy-start.2 = (bf16[2048,256]{0,1:T(8,128)(2,1)S(1)}, bf16[2048,256]{0,1:T(8,128)(2,1)}, u32[]{:S(2)}) copy-start(bf16[2048,256]{0,1:T(8,128)(2,1)} %all-gather.9.cloned.1.call-done) | copy-start | bytes 3145732
  440.1 91.5 %all-gather.11.cloned.1.call-start = ((), (), s32[]{:S(2)}) async-start(), calls=%async_computation.8 | async-start | bytes 2359296 | tf_op jit(solution)/shard_map/all_gather | solution.py:191
  481.6 50.1 %copy-start.4 = (f32[4,8]{1,0:T(4,128)S(1)}, f32[4,8]{1,0:T(4,128)}, u32[]{:S(2)}) copy-start(f32[4,8]{1,0:T(4,128)} %param.25) | copy-start | bytes 388
  481.6 50.7 %copy-start.5 = (bf16[512,1024]{1,0:T(8,128)(2,1)S(1)}, bf16[512,1024]{1,0:T(8,128)(2,1)}, u32[]{:S(2)}) copy-start(bf16[512,1024]{1,0:T(8,128)(2,1)} %param.24) | copy-start | bytes 3145732
  487.3 132.9 %reduce-scatter.8.cloned.1.call-start = ((), (), s32[]{:S(2)}) async-start(), calls=%async_computation.9 | async-start | bytes 4456448 | tf_op jit(solution)/shard_map/reduce_scatter | solution.py:193
Sparse Core Ops, SparseCore 0:
  29.5 55.0 all-gather.4
  91.9 43.6 reduce-scatter.3
  138.0 36.9 all-gather.8
  176.4 47.0 all-gather.6
  440.3 41.2 reduce-scatter.5
  487.4 44.1 all-gather.10
  538.4 81.7 reduce-scatter.7
where the time goes:
time: 628 us; the launch traced here: 627 us
  waiting for transfers between devices  332 us (53%)
  blocking collectives  83.6 us (13%)
  local copies, waits for them, and re-layouts  78.6 us (13%)
  matrix products  70.3 us (11%)
  other arithmetic  47 us (7%)
  between operations  14.4 us (2%)
    reduce_scatter x1, waiting for transfers between devices, body(): lax.psum_scatter(jnp.dot(attention_all, out_weight, preferred_element_typ...  81.9 us
    dynamic_slice x8, local copies, waits for them, and re-layouts, weighted_values(): return lax.scan(advance, start_state, (scores, value_blocks))[0]  65.5 us
    all_gather x1, waiting for transfers between devices, body(): gathered = lax.all_gather(normed, 'col', axis=0, tiled=True)  50.2 us
    all_gather x1, waiting for transfers between devices, body(): attention_all = lax.all_gather(attended, 'row', axis=0, tiled=True)  44.1 us
    reduce_scatter x1, waiting for transfers between devices, body(): lax.psum_scatter(jnp.dot(gathered, combined, preferred_element_type=jnp.f...  42.3 us
    reduce_scatter x1, waiting for transfers between devices, body(): lax.psum_scatter(cache_part.reshape(tokens, qwidth).astype(jnp.bfloat16),...  41.3 us
    all_gather x1, waiting for transfers between devices, body(): lax.all_gather(queries.reshape(tok_dev, qwidth), 'row', axis=0, tiled=True)  40.4 us
    dot_general x5, matrix products, advance(): jnp.einsum('htk,kd->thd', weights, block_item[1], preferred_element_type=...  35.5 us
  transfers between devices with their start and end apart: 7, of which 7 were waited for; matrix products, arithmetic and copies ran while one was open for 2% of the time, Pallas kernels for 0%

commit v1 on v0

--- a/solution.py
+++ b/solution.py
@@ -150,8 +150,11 @@
     cache_len = cache_dev * row_count
     cache_head = lax.dynamic_slice_in_dim(cache_keyval, kv_head * HD, HD, 2)
     span_index = cache_len + jnp.arange(tokens, dtype=jnp.int32)
-    all_queries = lax.all_gather(
-        queries.reshape(tok_dev, qwidth), "row", axis=0, tiled=True
+    all_queries = jnp.concatenate(
+        lax.all_to_all(
+            jnp.stack([queries.reshape(tok_dev, qwidth)] * lax.axis_size("row")), "row", 0, 0
+        ),
+        axis=0,
     ).reshape(tokens, heads_dev, HD)
     every_index = jnp.arange(tokens, dtype=jnp.int32)
     cache_index = row_index * cache_dev + jnp.arange(cache_dev, dtype=jnp.int32)

time: 628 us -> 594 us (0.946)
  waiting for transfers between devices: 332 us -> 281 us
  matrix products: 70.3 us -> 77.1 us
    all_gather x1 -> x0, waiting for transfers between devices: 40.4 us -> none  [body(): lax.all_gather(queries.reshape(tok_dev, qwidth), 'row', axis=0, tiled=True)]
    all_gather x1, waiting for transfers between devices: 31.9 us -> 0.02 us  [body(): lax.all_gather(jnp.concatenate([own_keys, own_values], axis=1), 'row', ax...]
    all_to_all x0 -> x1, waiting for transfers between devices: none -> 20.6 us  [body(): lax.all_to_all(jnp.stack([queries.reshape(tok_dev, qwidth)] * lax.axis_si...]
    dot_general x5, matrix products: 21.7 us -> 28.2 us  [block_scores(): jnp.einsum('thd,kd->htk', queries, key_block, preferred_element_type=jnp....]
  transfers between devices with their start and end apart: 7 -> 7, of which waited for: 7 -> 6; matrix products, arithmetic and copies ran while one was open for 2% -> 12% of each run, Pallas kernels for 0% -> 0%
where the time goes in v1:
time: 594 us; the launch traced here: 593 us
  waiting for transfers between devices  281 us (47%)
  local copies, waits for them, and re-layouts  83.7 us (14%)
  blocking collectives  83 us (14%)
  matrix products  77.1 us (13%)
  other arithmetic  49.2 us (8%)
  between operations  14.5 us (2%)
    reduce_scatter x1, waiting for transfers between devices, body(): lax.psum_scatter(jnp.dot(attention_all, out_weight, preferred_element_typ...  81.9 us
    dynamic_slice x8, local copies, waits for them, and re-layouts, weighted_values(): return lax.scan(advance, start_state, (scores, value_blocks))[0]  65.5 us
    all_gather x1, waiting for transfers between devices, body(): gathered = lax.all_gather(normed, 'col', axis=0, tiled=True)  50.2 us
    all_gather x1, waiting for transfers between devices, body(): attention_all = lax.all_gather(attended, 'row', axis=0, tiled=True)  44.3 us
    reduce_scatter x1, waiting for transfers between devices, body(): lax.psum_scatter(jnp.dot(gathered, combined, preferred_element_type=jnp.f...  42.6 us
    reduce_scatter x1, waiting for transfers between devices, body(): lax.psum_scatter(cache_part.reshape(tokens, qwidth).astype(jnp.bfloat16),...  41 us
    dot_general x5, matrix products, advance(): jnp.einsum('htk,kd->thd', weights, block_item[1], preferred_element_type=...  35.5 us
    pmax x1, blocking collectives, body(): lax.pmax(jnp.maximum(cache_peak, placed_peak).astype(jnp.bfloat16), 'row')  32.6 us
  transfers between devices with their start and end apart: 7, of which 6 were waited for; matrix products, arithmetic and copies ran while one was open for 12% of the time, Pallas kernels for 0%

profile of v1, /device:TPU:0, one launch (start us, length us, event | category | flops | bytes accessed | tf_op | source)
XLA Modules:
  0.0 592.6 jit_solution(13343225604243025345)
XLA Ops:
  6.5 1.2 fusion.27
  7.7 19.8 %psum.14 = f32[128]{0:T(128)S(1)} all-reduce(f32[128]{0:T(128)S(1)} %fusion.27), channel_id=1, replica_groups=mesh['row'=8,'col'=16] {'row'}, use_global_device_ids=true, to_apply=%region_1.0 | all-reduce | flops 128 | bytes 1024 | tf_op jit(solution)/shard_map/psum | solution.py:100
  27.5 1.8 fusion.29
  29.4 0.8 copy.38
  30.2 1.0 dynamic-slice_reduce_fusion.1
  31.2 1.4 multiply_convert_fusion.1
  32.7 1.2 broadcast_in_dim.164
  33.9 0.4 fusion.16
  34.3 50.2 %all-gather.4.cloned.1.call-done = bf16[2048,1024]{1,0:T(8,128)(2,1)} async-done(((bf16[128,1024]{1,0:T(8,128)(2,1)}), bf16[2048,1024]{1,0:T(8,128)(2,1)}) %all-gather.4.cloned.1.call-update) | async-done | bytes 4194320 | tf_op jit(solution)/shard_map/all_gather | solution.py:103
  84.6 7.2 %convolution_convert_fusion.1 = bf16[2048,768]{0,1:T(8,128)(2,1)} fusion(bf16[2048,1024]{1,0:T(8,128)(2,1)} %all-gather.4.cloned.1.call-done, bf16[1024,128]{1,0:T(8,128)(2,1)S(1)} %get-tuple-element.275, bf16[1024,128]{1,0:T(8,128)(2,1)S(1)} %get-tuple-element.274, bf16[1024,512]{1,0:T(8,128)(2,1)S(1)} %fusion.16), kind=kOutput, calls=%fused_computation.27 | convolution fusion | flops 3227516928 | bytes 8912896 | tf_op jit(solution)/shard_map/dot_general | solution.py:126
  92.5 0.5 multiply_cosine_fusion
  93.0 42.6 %reduce-scatter.4.cloned.1.call-done = bf16[256,768]{0,1:T(8,128)(2,1)} async-done(((bf16[2048,768]{0,1:T(8,128)(2,1)}), bf16[256,768]{0,1:T(8,128)(2,1)}) %reduce-scatter.4.cloned.1.call-update) | async-done | bytes 393232 | tf_op jit(solution)/shard_map/reduce_scatter | solution.py:125
  135.7 1.0 convert_element_type.106
  137.8 1.5 stack.3
  139.3 3.7 all-to-all-start
  143.0 0.8 fusion.47
  143.8 1.9 constant_dynamic-slice_fusion.4
  145.7 1.4 fusion.17
  147.2 0.3 fusion.38
  147.6 0.6 pad_maximum_fusion
  148.5 20.6 %all-to-all-done = bf16[8,256,512]{1,2,0:T(8,128)(2,1)S(1)} async-done(((bf16[8,256,512]{1,2,0:T(8,128)(2,1)}), bf16[8,256,512]{1,2,0:T(8,128)(2,1)S(1)}, u32[]{:S(2)}, u32[]{:S(2)}) %all-to-all-start) | async-done | bytes 2097184 | tf_op jit(solution)/shard_map/all_to_all | solution.py:154
  169.1 2.5 copy.43
  171.6 4.2 reshape_reshape.3
  175.8 3.0 copy.44
  178.8 27.7 %while.34 = (s32[]{:T(128)}, f32[4,4,2048,256]{2,3,1,0:T(8,128)}, s32[4,256]{1,0:T(4,128)S(1)}, s32[]{:T(128)}, bf16[4,256,128]{2,1,0:T(8,128)(2,1)}, /*index=5*/bf16[2048,4,128]{2,0,1:T(8,128)(2,1)S(1)}) while((s32[]{:T(128)}, f32[4,4,2048,256]{2,3,1,0:T(8,128)}, s32[4,256]{1,0:T(4,128)S(1)}, s32[]{:T(128)}, ...), condition=%wide.region_4.5_spmd.clone.clone, body=%wide.region_3.4_spmd.clone.sunk.clone | while | flops 542114560 | bytes 11606097 | solution.py:56
  178.8 0.7 compare_reduce_fusion.4
  179.5 0.6 fusion.64
  180.2 5.6 bitcast_dynamic-update-slice_fusion.3
  185.8 0.7 compare_reduce_fusion.4
  186.5 0.6 fusion.64
  187.1 5.6 bitcast_dynamic-update-slice_fusion.3
  192.7 0.7 compare_reduce_fusion.4
  193.4 0.6 fusion.64
  194.0 5.6 bitcast_dynamic-update-slice_fusion.3
  199.6 0.7 compare_reduce_fusion.4
  200.3 0.6 fusion.64
  200.9 5.6 bitcast_dynamic-update-slice_fusion.3
  206.5 12.0 %reduce_max.18 = f32[4,2048]{1,0:T(4,128)S(1)} reduce(f32[4,4,2048,256]{2,3,1,0:T(8,128)} %get-tuple-element.426, f32[]{:T(128)} %constant.145.clone.1), dimensions={0,3}, to_apply=%region_5.6 | reduce | flops 8380416 | bytes 33587204 | tf_op jit(solution)/shard_map/reduce_max | solution.py:60
  218.5 14.1 %select_reduce_fusion = f32[4,2048]{1,0:T(4,128)S(1)} fusion(f32[4,4,2048,256]{2,3,1,0:T(8,128)} %get-tuple-element.426, f32[4,2048]{1,0:T(4,128)S(1)} %reduce_max.18), kind=kLoop, calls=%fused_computation.20 | loop fusion | flops 33546240 | bytes 33619968 | tf_op jit(solution)/shard_map/reduce_sum | solution.py:62
  232.6 5.7 fusion.13
  238.4 32.6 %pmax.7 = bf16[4,2048]{1,0:T(4,128)(2,1)S(1)} all-reduce(bf16[4,2048]{1,0:T(4,128)(2,1)S(1)} %max.7), channel_id=1, replica_groups=mesh['row'=8,'col'=16] {'row'}, use_global_device_ids=true, to_apply=%region_7.8 | all-reduce | flops 8192 | bytes 32768 | tf_op jit(solution)/shard_map/pmax | solution.py:173
  271.0 4.6 select_reduce_fusion.1
  275.7 30.6 %psum.15 = bf16[4,2048]{1,0:T(4,128)(2,1)S(1)} all-reduce(bf16[4,2048]{1,0:T(4,128)(2,1)S(1)} %convert_element_type.114), channel_id=1, replica_groups=mesh['row'=8,'col'=16] {'row'}, use_global_device_ids=true, to_apply=%region_10.11 | all-reduce | flops 8192 | bytes 32768 | tf_op jit(solution)/shard_map/psum | solution.py:180
  306.4 95.3 %while.35 = (s32[]{:T(128)}, f32[2048,4,128]{0,2,1:T(8,128)}, bf16[4,256,128]{2,1,0:T(8,128)(2,1)}, f32[4,4,2048,256]{2,3,1,0:T(8,128)}, f32[4,2048]{1,0:T(4,128)S(1)}, /*index=5*/f32[4,2048]{1,0:T(4,128)S(1)}) while((s32[]{:T(128)}, f32[2048,4,128]{0,2,1:T(8,128)}, bf16[4,256,128]{2,1,0:T(8,128)(2,1)}, ...), condition=%wide.region_12.13_spmd.clone.clone, body=%wide.region_11.12_spmd.clone.sunk.clone | while | flops 545259520 | bytes 50463312 | solution.py:79
  306.4 7.7 %constant_dynamic-slice_fusion.8 = f32[1,4,2048,256]{2,3,1,0:T(8,128)} fusion(f32[4,4,2048,256]{2,3,1,0:T(8,128)} %get-tuple-element.438, s32[]{:T(128)} %get-tuple-element.429), kind=kLoop, calls=%fused_computation.7.clone.1.clone | loop fusion | bytes 16777220 | tf_op jit(solution)/shard_map/while/body/jit(dynamic_index_in_dim)/dynamic_slice | solution.py:79
  314.1 8.7 %copy.64 = f32[1,4,2048,256]{3,2,1,0:T(8,128)} copy(f32[1,4,2048,256]{2,3,1,0:T(8,128)} %constant_dynamic-slice_fusion.8) | data formatting | bytes 16777216 | tf_op jit(solution)/shard_map/while/body/jit(dynamic_index_in_dim)/dynamic_slice | solution.py:79
  322.7 6.8 %bitcast_add_fusion.3 = f32[2048,4,128]{0,2,1:T(8,128)} fusion(f32[2048,4,128]{0,2,1:T(8,128)} %get-tuple-element.430, f32[4,2048]{1,0:T(4,128)S(1)} %get-tuple-element.440, f32[1,4,2048,256]{3,2,1,0:T(8,128)} %copy.64, f32[4,2048]{1,0:T(4,128)S(1)} %get-tuple-element.439, pred[]{:T(512)S(6)} %compare.8, ...), kind=kOutput, calls=%fused_computation.2.clone.1.clone | convolution fusion | flops 545259520 | bytes 16908800 | tf_op jit(solution)/shard_map/while/body/eval_jaxpr/htk,kd->thd/dot_general | solution.py:74
  329.6 7.7 %constant_dynamic-slice_fusion.8 = f32[1,4,2048,256]{2,3,1,0:T(8,128)} fusion(f32[4,4,2048,256]{2,3,1,0:T(8,128)} %get-tuple-element.438, s32[]{:T(128)} %get-tuple-element.429), kind=kLoop, calls=%fused_computation.7.clone.1.clone | loop fusion | bytes 16777220 | tf_op jit(solution)/shard_map/while/body/jit(dynamic_index_in_dim)/dynamic_slice | solution.py:79
  337.2 8.7 %copy.64 = f32[1,4,2048,256]{3,2,1,0:T(8,128)} copy(f32[1,4,2048,256]{2,3,1,0:T(8,128)} %constant_dynamic-slice_fusion.8) | data formatting | bytes 16777216 | tf_op jit(solution)/shard_map/while/body/jit(dynamic_index_in_dim)/dynamic_slice | solution.py:79
  345.9 7.7 %bitcast_add_fusion.3 = f32[2048,4,128]{0,2,1:T(8,128)} fusion(f32[2048,4,128]{0,2,1:T(8,128)} %get-tuple-element.430, f32[4,2048]{1,0:T(4,128)S(1)} %get-tuple-element.440, f32[1,4,2048,256]{3,2,1,0:T(8,128)} %copy.64, f32[4,2048]{1,0:T(4,128)S(1)} %get-tuple-element.439, pred[]{:T(512)S(6)} %compare.8, ...), kind=kOutput, calls=%fused_computation.2.clone.1.clone | convolution fusion | flops 545259520 | bytes 16908800 | tf_op jit(solution)/shard_map/while/body/eval_jaxpr/htk,kd->thd/dot_general | solution.py:74
  353.6 7.7 %constant_dynamic-slice_fusion.8 = f32[1,4,2048,256]{2,3,1,0:T(8,128)} fusion(f32[4,4,2048,256]{2,3,1,0:T(8,128)} %get-tuple-element.438, s32[]{:T(128)} %get-tuple-element.429), kind=kLoop, calls=%fused_computation.7.clone.1.clone | loop fusion | bytes 16777220 | tf_op jit(solution)/shard_map/while/body/jit(dynamic_index_in_dim)/dynamic_slice | solution.py:79
  361.3 8.7 %copy.64 = f32[1,4,2048,256]{3,2,1,0:T(8,128)} copy(f32[1,4,2048,256]{2,3,1,0:T(8,128)} %constant_dynamic-slice_fusion.8) | data formatting | bytes 16777216 | tf_op jit(solution)/shard_map/while/body/jit(dynamic_index_in_dim)/dynamic_slice | solution.py:79
  369.9 7.7 %bitcast_add_fusion.3 = f32[2048,4,128]{0,2,1:T(8,128)} fusion(f32[2048,4,128]{0,2,1:T(8,128)} %get-tuple-element.430, f32[4,2048]{1,0:T(4,128)S(1)} %get-tuple-element.440, f32[1,4,2048,256]{3,2,1,0:T(8,128)} %copy.64, f32[4,2048]{1,0:T(4,128)S(1)} %get-tuple-element.439, pred[]{:T(512)S(6)} %compare.8, ...), kind=kOutput, calls=%fused_computation.2.clone.1.clone | convolution fusion | flops 545259520 | bytes 16908800 | tf_op jit(solution)/shard_map/while/body/eval_jaxpr/htk,kd->thd/dot_general | solution.py:74
  377.6 7.7 %constant_dynamic-slice_fusion.8 = f32[1,4,2048,256]{2,3,1,0:T(8,128)} fusion(f32[4,4,2048,256]{2,3,1,0:T(8,128)} %get-tuple-element.438, s32[]{:T(128)} %get-tuple-element.429), kind=kLoop, calls=%fused_computation.7.clone.1.clone | loop fusion | bytes 16777220 | tf_op jit(solution)/shard_map/while/body/jit(dynamic_index_in_dim)/dynamic_slice | solution.py:79
  385.3 8.7 %copy.64 = f32[1,4,2048,256]{3,2,1,0:T(8,128)} copy(f32[1,4,2048,256]{2,3,1,0:T(8,128)} %constant_dynamic-slice_fusion.8) | data formatting | bytes 16777216 | tf_op jit(solution)/shard_map/while/body/jit(dynamic_index_in_dim)/dynamic_slice | solution.py:79
  394.0 7.7 %bitcast_add_fusion.3 = f32[2048,4,128]{0,2,1:T(8,128)} fusion(f32[2048,4,128]{0,2,1:T(8,128)} %get-tuple-element.430, f32[4,2048]{1,0:T(4,128)S(1)} %get-tuple-element.440, f32[1,4,2048,256]{3,2,1,0:T(8,128)} %copy.64, f32[4,2048]{1,0:T(4,128)S(1)} %get-tuple-element.439, pred[]{:T(512)S(6)} %compare.8, ...), kind=kOutput, calls=%fused_computation.2.clone.1.clone | convolution fusion | flops 545259520 | bytes 16908800 | tf_op jit(solution)/shard_map/while/body/eval_jaxpr/htk,kd->thd/dot_general | solution.py:74
  401.7 3.9 convert_element_type.116
  405.6 0.3 all-gather.8.cloned.1.call-start
  405.9 41.0 %reduce-scatter.6.cloned.1.call-done = bf16[256,512]{0,1:T(8,128)(2,1)} async-done(((bf16[2048,512]{0,1:T(8,128)(2,1)}), bf16[256,512]{0,1:T(8,128)(2,1)}) %reduce-scatter.6.cloned.1.call-update) | async-done | bytes 262160 | tf_op jit(solution)/shard_map/reduce_scatter | solution.py:185
  446.9 5.6 fusion.25
  452.6 44.3 %all-gather.8.cloned.1.call-done = bf16[2048,512]{0,1:T(8,128)(2,1)} async-done(((bf16[256,512]{0,1:T(8,128)(2,1)}), bf16[2048,512]{0,1:T(8,128)(2,1)}) %all-gather.8.cloned.1.call-update) | async-done | bytes 2097168 | tf_op jit(solution)/shard_map/all_gather | solution.py:194
  496.9 0.6 broadcast_in_dim.176
  497.5 6.2 %convolution_convert_fusion = bf16[2048,1024]{1,0:T(8,128)(2,1)} fusion(bf16[2048,512]{0,1:T(8,128)(2,1)} %all-gather.8.cloned.1.call-done, f32[64,8,8,128]{3,2,1,0:T(8,128)S(1)} %bitcast.117, bf16[512,1024]{1,0:T(8,128)(2,1)} %param.24), kind=kOutput, calls=%fused_computation.26 | convolution fusion | flops 2151153664 | bytes 9437184 | tf_op jit(solution)/shard_map/dot_general | solution.py:197
  503.8 81.9 %reduce-scatter.8.cloned.1.call-done = bf16[128,1024]{1,0:T(8,128)(2,1)} async-done(((bf16[2048,1024]{1,0:T(8,128)(2,1)}), bf16[128,1024]{1,0:T(8,128)(2,1)}) %reduce-scatter.8.cloned.1.call-update) | async-done | bytes 262160 | tf_op jit(solution)/shard_map/reduce_scatter | solution.py:196
  (57 shorter events, 1.9 us)
Async XLA Ops:
  6.5 27.4 %copy-start.2 = (bf16[1024,512]{1,0:T(8,128)(2,1)S(1)}, bf16[1024,512]{1,0:T(8,128)(2,1)}, u32[]{:S(2)}) copy-start(bf16[1024,512]{1,0:T(8,128)(2,1)} %param.18) | copy-start | bytes 3145732
  6.5 78.0 %all-gather.4.cloned.1.call-start = ((), (), s32[]{:S(2)}) async-start(), calls=%async_computation.4 | async-start | bytes 4456448 | tf_op jit(solution)/shard_map/all_gather | solution.py:103
  29.3 106.3 %reduce-scatter.4.cloned.1.call-start = ((), (), s32[]{:S(2)}) async-start(), calls=%async_computation.5 | async-start | bytes 3538944 | tf_op jit(solution)/shard_map/reduce_scatter | solution.py:125
  91.8 44.9 %copy-start.4 = (f32[512]{0:T(512)S(1)}, f32[512]{0:T(512)}, u32[]{:S(2)}) copy-start(f32[512]{0:T(512)} %param.20) | copy-start | bytes 6148
  137.6 1.6 copy-start
  139.3 29.8 %all-to-all-start = ((bf16[8,256,512]{1,2,0:T(8,128)(2,1)}), bf16[8,256,512]{1,2,0:T(8,128)(2,1)S(1)}, u32[]{:S(2)}, u32[]{:S(2)}) async-start(bf16[8,256,512]{1,2,0:T(8,128)(2,1)} %stack.3), calls=%async_computation.1 | async-start | bytes 4194304 | tf_op jit(solution)/shard_map/all_to_all | solution.py:154
  142.9 89.7 %all-gather.6.cloned.1.call-start = ((), (), s32[]{:S(2)}) async-start(), calls=%async_computation.6 | async-start | bytes 1179648 | tf_op jit(solution)/shard_map/all_gather | solution.py:144
  148.2 298.6 %reduce-scatter.6.cloned.1.call-start = ((), (), s32[]{:S(2)}) async-start(), calls=%async_computation.7 | async-start | bytes 2359296 | tf_op jit(solution)/shard_map/reduce_scatter | solution.py:185
  218.5 14.1 %copy-start.1 = (bf16[256,4,128]{2,0,1:T(8,128)(2,1)S(1)}, bf16[256,4,128]{2,0,1:T(8,128)(2,1)}, u32[]{:S(2)}) copy-start(bf16[256,4,128]{2,0,1:T(8,128)(2,1)} %copy-done) | copy-start | bytes 786436
  401.7 45.2 %copy-start.3 = (bf16[2048,256]{0,1:T(8,128)(2,1)S(1)}, bf16[2048,256]{0,1:T(8,128)(2,1)}, u32[]{:S(2)}) copy-start(bf16[2048,256]{0,1:T(8,128)(2,1)} %all-gather.6.cloned.1.call-done) | copy-start | bytes 3145732
  405.6 91.3 %all-gather.8.cloned.1.call-start = ((), (), s32[]{:S(2)}) async-start(), calls=%async_computation.8 | async-start | bytes 2359296 | tf_op jit(solution)/shard_map/all_gather | solution.py:194
  446.9 50.0 %copy-start.5 = (f32[4,8]{1,0:T(4,128)S(1)}, f32[4,8]{1,0:T(4,128)}, u32[]{:S(2)}) copy-start(f32[4,8]{1,0:T(4,128)} %param.25) | copy-start | bytes 388
  452.5 133.2 %reduce-scatter.8.cloned.1.call-start = ((), (), s32[]{:S(2)}) async-start(), calls=%async_computation.9 | async-start | bytes 4456448 | tf_op jit(solution)/shard_map/reduce_scatter | solution.py:196
Sparse Core Ops, SparseCore 0:
  29.5 55.0 all-gather.3
  91.9 43.6 reduce-scatter.3
  148.4 41.5 all-gather.5
  405.7 41.0 reduce-scatter.5
  452.7 44.1 all-gather.7
  503.9 81.7 reduce-scatter.7
